TPU v7x, 32 devices: a whole 2x2x4 slice. The times are simulated.
32 devices in a mesh: chan: 8 (over z, x), seg: 4 (over y, core).
Axes of the slice: x: 2, y: 2, z: 4, core: 2. Of those that a mesh axis runs over, the one named last changes fastest.
Arguments:
- spectra: bfloat16 [32, 128, 2, 1024], P(None, 'seg', None, 'chan'), may hold values from -6 to 6
- plan: int32 [4, 8], replicated, may hold values from 0 to 7, as said below
- assignment: int32 [1024], P('chan'), may hold values from 0 to 1023, as said below
Outputs:
- cross_spectra: float32 [4, 32, 2, 1024, 128], P(None, 'seg', None, 'chan')
Inputs may be any that keep to these rules, and one draw needn't show every extreme that they name: Each row is a pairing of the blocks: plan[r, plan[r, b]] = b and plan[r, b] != b; no two blocks are paired in two different rounds. `assignment`: entries b * 128 to (b + 1) * 128 - 1 are a permutation of that same range of channels.
All inputs are finite; a program needn't handle non-finite values.
Results may differ from a plain program's by a relative error of at most 0.0003.
Values may be sent and summed in bfloat16 or wider, within the bound.
A program may use at most 128 MiB of HBM per device.

v0:
```python
import math

import jax
import jax.numpy as jnp
from jax import lax
from jax.sharding import PartitionSpec as P


def cross_block(own_rows, other_rows, chan_width):
    product = jnp.einsum("fwa,fwb->fab", own_rows, other_rows, preferred_element_type=jnp.float32)
    real_part = product[:, :chan_width, :chan_width] + product[:, chan_width:, chan_width:]
    imag_part = product[:, chan_width:, :chan_width] - product[:, :chan_width, chan_width:]
    return jnp.stack([real_part, imag_part], axis=1)


def on_device(spectra, plan, assignment):
    chan_width = spectra.shape[3]
    scale = 1.0 / math.sqrt(spectra.shape[1] * lax.axis_size("seg"))
    local_slots = assignment - lax.axis_index("chan") * chan_width
    ordered = jnp.take(spectra, local_slots, axis=3)
    bin_count = ordered.shape[0]
    win_count = ordered.shape[1]
    group_count = lax.axis_size("chan")
    piece_rows = bin_count * win_count // group_count
    own_rows = ordered.reshape(bin_count, win_count, 2 * chan_width)
    pieces = ordered.reshape(group_count, piece_rows, 2 * chan_width)
    held = lax.all_to_all(pieces, "chan", split_axis=0, concat_axis=0, tiled=True)
    results = []
    for round_index in range(plan.shape[0]):
        outgoing = jnp.take(held, plan[round_index], axis=0)
        arrived = lax.all_to_all(outgoing, "chan", split_axis=0, concat_axis=0, tiled=True)
        other_rows = arrived.reshape(bin_count, win_count, 2 * chan_width)
        block_result = cross_block(own_rows, other_rows, chan_width) * scale
        results.append(block_result)
    stacked = jnp.stack(results)
    return lax.psum_scatter(stacked, "seg", scatter_dimension=1, tiled=True)


def solution(mesh):
    in_specs = (P(None, "seg", None, "chan"), P(), P("chan"))
    out_specs = P(None, "seg", None, "chan", None)
    return jax.shard_map(
        on_device, mesh=mesh, in_specs=in_specs, out_specs=out_specs, check_vma=False
    )
```

profile of v0, /device:TPU:0, one launch (start us, length us, event | category | flops | bytes accessed | tf_op | source)
XLA Modules:
  0.0 281.6 jit_solution(7640039450648420011)
XLA Ops:
  6.5 0.7 compare_and_fusion.4
  7.2 0.0 copy-start.5
  7.2 3.5 %copy.11 = bf16[32,32,2,128]{1,0,2,3:T(8,128)(2,1)S(1)} copy(bf16[32,32,2,128]{3,2,1,0:T(2,128)(2,1)} %param.5) | data formatting | bytes 1048576 | tf_op args[0]
  10.7 2.1 gather_fusion
  12.8 3.5 %copy.12 = bf16[32,32,2,128]{3,2,1,0:T(2,128)(2,1)S(1)} copy(bf16[32,32,2,128]{1,0,2,3:T(8,128)(2,1)} %bitcast.58) | data formatting | bytes 1048576 | tf_op jit(solution)/shard_map/jit(_take)/gather | solution.py:20
  16.3 0.3 gather.13
  16.7 0.8 broadcast_select_fusion.4
  17.5 7.3 %all-to-all-start = ((bf16[8,128,256]{2,1,0:T(8,128)(2,1)}), bf16[8,128,256]{2,1,0:T(8,128)(2,1)S(1)}, u32[]{:S(2)}, u32[]{:S(2)}) async-start(bf16[8,128,256]{2,1,0:T(8,128)(2,1)} %broadcast_select_fusion.4), calls=%async_computation | async-start | bytes 1048576 | tf_op jit(solution)/shard_map/all_to_all | solution.py:27
  24.8 0.0 copy-done.5
  24.8 14.4 %all-to-all-done = bf16[8,128,256]{2,1,0:T(8,128)(2,1)S(1)} async-done(((bf16[8,128,256]{2,1,0:T(8,128)(2,1)}), bf16[8,128,256]{2,1,0:T(8,128)(2,1)S(1)}, u32[]{:S(2)}, u32[]{:S(2)}) %all-to-all-start) | async-done | bytes 524320 | tf_op jit(solution)/shard_map/all_to_all | solution.py:27
  39.3 0.6 gather_fusion.2
  39.9 0.9 broadcast_select_fusion.2
  40.8 3.6 %all-to-all-start.2 = ((bf16[8,128,256]{2,1,0:T(8,128)(2,1)}), bf16[8,128,256]{2,1,0:T(8,128)(2,1)S(1)}, u32[]{:S(2)}, u32[]{:S(2)}) async-start(bf16[8,128,256]{2,1,0:T(8,128)(2,1)} %broadcast_select_fusion.2), calls=%async_computation.2 | async-start | bytes 1048576 | tf_op jit(solution)/shard_map/all_to_all | solution.py:31
  44.4 0.6 gather_fusion.1
  45.0 0.9 broadcast_select_fusion.3
  45.9 13.1 %all-to-all-done.2 = bf16[8,128,256]{2,1,0:T(8,128)(2,1)S(1)} async-done(((bf16[8,128,256]{2,1,0:T(8,128)(2,1)}), bf16[8,128,256]{2,1,0:T(8,128)(2,1)S(1)}, u32[]{:S(2)}, u32[]{:S(2)}) %all-to-all-start.2) | async-done | bytes 524320 | tf_op jit(solution)/shard_map/all_to_all | solution.py:31
  59.1 3.6 %all-to-all-start.1 = ((bf16[8,128,256]{2,1,0:T(8,128)(2,1)}), bf16[8,128,256]{2,1,0:T(8,128)(2,1)S(1)}, u32[]{:S(2)}, u32[]{:S(2)}) async-start(bf16[8,128,256]{2,1,0:T(8,128)(2,1)} %broadcast_select_fusion.3), calls=%async_computation.1 | async-start | bytes 1048576 | tf_op jit(solution)/shard_map/all_to_all | solution.py:31
  62.7 0.3 gather.12
  63.1 0.6 gather_fusion.4
  63.7 0.6 gather_fusion.3
  64.2 0.9 broadcast_select_fusion
  65.2 0.9 broadcast_select_fusion.1
  66.1 11.3 %all-to-all-done.1 = bf16[8,128,256]{2,1,0:T(8,128)(2,1)S(1)} async-done(((bf16[8,128,256]{2,1,0:T(8,128)(2,1)}), bf16[8,128,256]{2,1,0:T(8,128)(2,1)S(1)}, u32[]{:S(2)}, u32[]{:S(2)}) %all-to-all-start.1) | async-done | bytes 524320 | tf_op jit(solution)/shard_map/all_to_all | solution.py:31
  77.4 4.2 %all-to-all-start.3 = ((bf16[8,128,256]{2,1,0:T(8,128)(2,1)}), bf16[8,128,256]{2,1,0:T(8,128)(2,1)}, u32[]{:S(2)}, u32[]{:S(2)}) async-start(bf16[8,128,256]{2,1,0:T(8,128)(2,1)} %broadcast_select_fusion.1), calls=%async_computation.3 | async-start | bytes 1048576 | tf_op jit(solution)/shard_map/all_to_all | solution.py:31
  81.5 1.3 fusion.11
  82.8 2.0 fusion.7
  84.8 4.5 %fusion.10 = f32[32,256,256]{2,1,0:T(8,128)} fusion(bf16[32,32,256]{2,1,0:T(8,128)(2,1)S(1)} %bitcast.59, bf16[32,32,256]{2,1,0:T(8,128)(2,1)S(1)} %gather.12, pred[256]{0:T(512)(128)(4,1)S(1)} %broadcast_bitcast_fusion), kind=kOutput, calls=%fused_computation.35 | convolution fusion | flops 134479872 | bytes 9437440 | tf_op jit(solution)/shard_map/fwa,fwb->fab/dot_general | solution.py:10
  89.4 6.5 %all-to-all-done.3 = bf16[8,128,256]{2,1,0:T(8,128)(2,1)} async-done(((bf16[8,128,256]{2,1,0:T(8,128)(2,1)}), bf16[8,128,256]{2,1,0:T(8,128)(2,1)}, u32[]{:S(2)}, u32[]{:S(2)}) %all-to-all-start.3) | async-done | bytes 524320 | tf_op jit(solution)/shard_map/all_to_all | solution.py:31
  95.8 3.6 %all-to-all-start.4 = ((bf16[8,128,256]{2,1,0:T(8,128)(2,1)}), bf16[8,128,256]{2,1,0:T(8,128)(2,1)S(1)}, u32[]{:S(2)}, u32[]{:S(2)}) async-start(bf16[8,128,256]{2,1,0:T(8,128)(2,1)} %broadcast_select_fusion), calls=%async_computation.4 | async-start | bytes 1048576 | tf_op jit(solution)/shard_map/all_to_all | solution.py:31
  99.4 0.2 reduce-scatter.5.cloned.1.call-start
  99.7 6.7 %fusion.5 = (f32[1,32,1,128,128]{4,3,1,2,0:T(8,128)}, f32[1,32,1,128,128]{4,3,1,2,0:T(8,128)}) fusion(f32[32,256,256]{2,1,0:T(8,128)} %fusion.10), kind=kLoop, calls=%fused_computation.22 | loop fusion | flops 1048576 | bytes 12582912 | tf_op jit(solution)/shard_map/stack | solution.py:13
  106.4 2.3 fusion.9
  108.7 2.6 fusion.3
  111.3 2.6 all-to-all-done.4
  114.0 1.3 fusion.8
  115.2 0.0 copy-start
  115.3 0.0 copy-start.3
  115.3 0.0 copy-start.4
  115.3 0.6 fusion.1
  115.9 1.0 copy-done
  116.8 0.6 copy-done.3
  117.5 0.6 copy-done.4
  118.1 0.0 copy-start.1
  118.1 0.0 copy-start.2
  118.1 3.1 %maximum_multiply_fusion = (f32[1,32,2,128,128]{4,3,1,2,0:T(8,128)S(1)}, f32[1,32,2,128,128]{4,3,1,2,0:T(8,128)}) fusion(f32[1,32,1,128,128]{4,3,1,2,0:T(8,128)S(1)} %copy-done, f32[1,32,1,128,128]{4,3,1,2,0:T(8,128)S(1)} %get-tuple-element.16, f32[1,32,1,128,128]{4,3,1,2,0:T(8,128)S(1)} %copy-done.4, f32[1,32,1,128,128]{4,3,1,2,0:T(8,128)S(1)} %copy-done.3), kind=kLoop, calls=%fused_computation.7 | loop fusion | flops 4194304 | bytes 16777216 | tf_op jit(solution)/shard_map/mul | solution.py:33
  121.2 0.0 copy-done.1
  121.2 0.0 copy-done.2
  121.2 4.3 %maximum_multiply_fusion.2 = (f32[1,32,2,128,128]{4,3,1,2,0:T(8,128)}, f32[1,32,2,128,128]{4,3,1,2,0:T(8,128)}) fusion(f32[1,32,1,128,128]{4,3,1,2,0:T(8,128)S(1)} %copy-done.2, f32[1,32,1,128,128]{4,3,1,2,0:T(8,128)S(1)} %copy-done.1, f32[1,32,1,128,128]{4,3,1,2,0:T(8,128)S(1)} %get-tuple-element.23, f32[1,32,1,128,128]{4,3,1,2,0:T(8,128)S(1)} %get-tuple-element.22), kind=kLoop, calls=%fused_computation.9 | loop fusion | flops 4194304 | bytes 16777216 | tf_op jit(solution)/shard_map/mul | solution.py:33
  125.5 5.6 %pad_maximum_fusion = f32[4,32,2,128,128]{4,3,1,2,0:T(8,128)S(1)} fusion(f32[1,32,2,128,128]{4,3,1,2,0:T(8,128)} %get-tuple-element.33, f32[1,32,2,128,128]{4,3,1,2,0:T(8,128)} %get-tuple-element.32, f32[1,32,2,128,128]{4,3,1,2,0:T(8,128)} %get-tuple-element.31, f32[1,32,2,128,128]{4,3,1,2,0:T(8,128)S(1)} %get-tuple-element.30), kind=kLoop, calls=%fused_computation.6 | loop fusion | flops 12582912 | bytes 33554432 | tf_op jit(solution)/shard_map/stack | solution.py:35
  131.1 1.6 copy.15
  132.7 11.7 %copy.22 = f32[4,8,1024,128]{3,1,2,0:T(8,128)} copy(f32[4,8,1024,128]{3,2,1,0:T(8,128)S(1)} %bitcast.56) | data formatting | bytes 33554432
  144.5 0.0 reduce-scatter.5.cloned.1.call-update
  144.5 125.3 %reduce-scatter.5.cloned.1.call-done = f32[8,131072]{1,0:T(8,128)} async-done(((f32[32,131072]{1,0:T(8,128)}), f32[8,131072]{1,0:T(8,128)}) %reduce-scatter.5.cloned.1.call-update) | async-done | bytes 4194320
  269.8 4.9 %copy.14 = f32[4,8,2,128,128]{4,3,2,1,0:T(8,128)} copy(f32[4,8,2,128,128]{4,1,3,2,0:T(8,128)} %bitcast.57) | data formatting | bytes 8388608 | tf_op jit(solution)/shard_map/reduce_scatter | solution.py:36
  (7 shorter events, 0.0 us)
Async XLA Ops:
  7.2 17.6 %copy-start.5 = (s32[4,8]{1,0:T(4,128)S(1)}, s32[4,8]{1,0:T(4,128)}, u32[]{:S(2)}) copy-start(s32[4,8]{1,0:T(4,128)} %param.6) | copy-start | bytes 388
  17.5 21.7 %all-to-all-start = ((bf16[8,128,256]{2,1,0:T(8,128)(2,1)}), bf16[8,128,256]{2,1,0:T(8,128)(2,1)S(1)}, u32[]{:S(2)}, u32[]{:S(2)}) async-start(bf16[8,128,256]{2,1,0:T(8,128)(2,1)} %broadcast_select_fusion.4), calls=%async_computation | async-start | bytes 1048576 | tf_op jit(solution)/shard_map/all_to_all | solution.py:27
  40.8 18.3 %all-to-all-start.2 = ((bf16[8,128,256]{2,1,0:T(8,128)(2,1)}), bf16[8,128,256]{2,1,0:T(8,128)(2,1)S(1)}, u32[]{:S(2)}, u32[]{:S(2)}) async-start(bf16[8,128,256]{2,1,0:T(8,128)(2,1)} %broadcast_select_fusion.2), calls=%async_computation.2 | async-start | bytes 1048576 | tf_op jit(solution)/shard_map/all_to_all | solution.py:31
  59.1 18.3 %all-to-all-start.1 = ((bf16[8,128,256]{2,1,0:T(8,128)(2,1)}), bf16[8,128,256]{2,1,0:T(8,128)(2,1)S(1)}, u32[]{:S(2)}, u32[]{:S(2)}) async-start(bf16[8,128,256]{2,1,0:T(8,128)(2,1)} %broadcast_select_fusion.3), calls=%async_computation.1 | async-start | bytes 1048576 | tf_op jit(solution)/shard_map/all_to_all | solution.py:31
  77.4 18.5 %all-to-all-start.3 = ((bf16[8,128,256]{2,1,0:T(8,128)(2,1)}), bf16[8,128,256]{2,1,0:T(8,128)(2,1)}, u32[]{:S(2)}, u32[]{:S(2)}) async-start(bf16[8,128,256]{2,1,0:T(8,128)(2,1)} %broadcast_select_fusion.1), calls=%async_computation.3 | async-start | bytes 1048576 | tf_op jit(solution)/shard_map/all_to_all | solution.py:31
  95.8 18.1 %all-to-all-start.4 = ((bf16[8,128,256]{2,1,0:T(8,128)(2,1)}), bf16[8,128,256]{2,1,0:T(8,128)(2,1)S(1)}, u32[]{:S(2)}, u32[]{:S(2)}) async-start(bf16[8,128,256]{2,1,0:T(8,128)(2,1)} %broadcast_select_fusion), calls=%async_computation.4 | async-start | bytes 1048576 | tf_op jit(solution)/shard_map/all_to_all | solution.py:31
  99.4 170.4 %reduce-scatter.5.cloned.1.call-start = ((), (), s32[]{:S(2)}) async-start(), calls=%async_computation.6 | async-start | bytes 20971520
  115.2 1.6 copy-start
  115.3 2.2 copy-start.3
  115.3 2.8 %copy-start.4 = (f32[1,32,1,128,128]{4,3,1,2,0:T(8,128)S(1)}, f32[1,32,1,128,128]{4,3,1,2,0:T(8,128)}, u32[]{:S(2)}) copy-start(f32[1,32,1,128,128]{4,3,1,2,0:T(8,128)} %get-tuple-element.19) | copy-start | bytes 6291460
  118.1 3.1 %copy-start.1 = (f32[1,32,1,128,128]{4,3,1,2,0:T(8,128)S(1)}, f32[1,32,1,128,128]{4,3,1,2,0:T(8,128)}, u32[]{:S(2)}) copy-start(f32[1,32,1,128,128]{4,3,1,2,0:T(8,128)} %get-tuple-element.20) | copy-start | bytes 6291460
  118.1 3.1 %copy-start.2 = (f32[1,32,1,128,128]{4,3,1,2,0:T(8,128)S(1)}, f32[1,32,1,128,128]{4,3,1,2,0:T(8,128)}, u32[]{:S(2)}) copy-start(f32[1,32,1,128,128]{4,3,1,2,0:T(8,128)} %get-tuple-element.21) | copy-start | bytes 6291460
Sparse Core Ops, SparseCore 0:
  144.6 125.1 reduce-scatter.4
where the time goes:
time: 282 us
  waiting for transfers between devices  173 us (61%)
  local copies, waits for them, and re-layouts  32.6 us (12%)
  other arithmetic  30.1 us (11%)
  starting transfers between devices  22.5 us (8%)
  between operations  13.6 us (5%)
  matrix products  9.46 us (3%)
    unnamed x2, waiting for transfers between devices  125 us
    all_to_all x4, waiting for transfers between devices, on_device(): lax.all_to_all(outgoing, 'chan', split_axis=0, concat_axis=0, tiled=True)  33.5 us
    unnamed x15, local copies, waits for them, and re-layouts  19 us
    all_to_all x4, starting transfers between devices, on_device(): lax.all_to_all(outgoing, 'chan', split_axis=0, concat_axis=0, tiled=True)  15 us
    all_to_all x1, waiting for transfers between devices, on_device(): lax.all_to_all(pieces, 'chan', split_axis=0, concat_axis=0, tiled=True)  14.4 us
    another operation x4, other arithmetic, cross_block(): return jnp.stack([real_part, imag_part], axis=1)  11.9 us
    dot_general x4, matrix products, cross_block(): jnp.einsum('fwa,fwb->fab', own_rows, other_rows, preferred_element_type=j...  9.46 us
    mul x2, other arithmetic, on_device(): block_result = cross_block(own_rows, other_rows, chan_width) * scale  7.42 us
  transfers between devices with their start and end apart: 6, of which 6 were waited for; matrix products, arithmetic and copies ran while one was open for 9% of the time, Pallas kernels for 0%

commit v1 on v0

v1 whole, which is shorter than its diff:
```python
import functools
import math

import jax
import jax.numpy as jnp
from jax import lax
from jax.experimental import pallas as pl
from jax.experimental.pallas import tpu as pltpu
from jax.sharding import PartitionSpec as P

MESH = pl.DeviceIdType.MESH


def ring_place(chan, n_chan):
    z, x = chan // 2, chan % 2
    return z + x * (n_chan - 1 - 2 * z)


def ring_chan(place, n_chan):
    x = place // (n_chan // 2)
    z = place + x * (n_chan - 1 - 2 * place)
    return 2 * z + x


def seg_peer(seg, step, n_seg):
    pair = (seg // 2 + step // 2) % (n_seg // 2)
    return 2 * pair + (seg % 2 + step) % 2


def gather_kernel(n_chan, n_seg, slots_ref, x_ref, out_ref, sorted_ref, own_sem, seg_send, seg_recv, ring_send, ring_recv):
    chan, seg = lax.axis_index("chan"), lax.axis_index("seg")
    place = ring_place(chan, n_chan)
    sides = (
        ring_chan((place + 1) % n_chan, n_chan),
        ring_chan((place + n_chan - 1) % n_chan, n_chan),
    )
    peers = [seg_peer(seg, step, n_seg) for step in range(n_seg)]
    _, bins, rows, width = sorted_ref.shape

    barrier = pltpu.get_barrier_semaphore()
    for side in sides:
        pl.semaphore_signal(barrier, inc=1, device_id=(side, seg), device_id_type=MESH)
    for peer in peers[1:]:
        pl.semaphore_signal(barrier, inc=1, device_id=(chan, peer), device_id_type=MESH)

    column = lax.broadcasted_iota(jnp.int32, (width, width), 0)
    pick = (column == slots_ref[...]).astype(jnp.float32).astype(jnp.bfloat16)

    def sort_part(step):
        part = x_ref[pl.ds(peers[step] * bins, bins)].reshape(bins * rows, width)
        part = jnp.dot(part, pick, preferred_element_type=jnp.float32)
        sorted_ref[step] = part.astype(jnp.bfloat16).reshape(bins, rows, width)

    hops = n_chan // 2

    def ring_copy(way, hop, part):
        held = (n_chan - hop) % n_chan if way else hop
        lands = n_chan - hop - 1 if way else hop + 1
        source = sorted_ref.at[0] if (hop, part) == (0, 0) else out_ref.at[held, part]
        return pltpu.make_async_remote_copy(
            src_ref=source,
            dst_ref=out_ref.at[lands, part],
            send_sem=ring_send.at[way, hop, part],
            recv_sem=ring_recv.at[way, hop, part],
            device_id=(sides[way], seg),
            device_id_type=MESH,
        )

    def goes(way, hop, part):
        return hop < hops - 1 or (part >= n_seg // 2) == bool(way)

    ring = {
        (way, hop, part): ring_copy(way, hop, part)
        for hop in range(hops)
        for part in range(n_seg)
        for way in range(2)
        if goes(way, hop, part)
    }
    swap = {
        step: pltpu.make_async_remote_copy(
            src_ref=sorted_ref.at[step],
            dst_ref=out_ref.at[0, step],
            send_sem=seg_send.at[step],
            recv_sem=seg_recv.at[step],
            device_id=(chan, peers[step]),
            device_id_type=MESH,
        )
        for step in range(1, n_seg)
    }

    sort_part(0)
    pl.semaphore_wait(barrier, 1 + n_seg)
    ring[0, 0, 0].start()
    ring[1, 0, 0].start()
    for step in list(range(2, n_seg)) + [1]:
        sort_part(step)
        swap[step].start()
    own = pltpu.make_async_copy(sorted_ref.at[0], out_ref.at[0, 0], own_sem)
    own.start()

    for hop in range(hops):
        for part in range(n_seg):
            if hop == 0 and part > 0:
                swap[part].wait_recv()
            for way in range(2):
                if (way, hop, part) in ring and (hop, part) != (0, 0):
                    if hop > 0:
                        ring[way, hop - 1, part].wait_recv()
                    ring[way, hop, part].start()
    own.wait()
    for step in range(1, n_seg):
        swap[step].wait_send()
    for (way, hop, part), copy in ring.items():
        if (way, hop + 1, part) not in ring:
            copy.wait_recv()
        copy.wait_send()


def cross_kernel(scale, held_ref, own_ref, other_ref, out_ref, left_ref):
    _, parts, bins, rows, width = own_ref.shape
    depth = parts * rows

    @pl.when(pl.program_id(0) == 0)
    def _():
        row = lax.broadcasted_iota(jnp.int32, (depth, depth), 0)
        col = lax.broadcasted_iota(jnp.int32, (depth, depth), 1)
        up = ((row % 2 == 0) & (col == row + 1)).astype(jnp.float32)
        down = ((row % 2 == 1) & (col == row - 1)).astype(jnp.float32)
        turn = (up - down).astype(jnp.bfloat16)
        for b in range(bins):
            x = own_ref[0, :, b].reshape(depth, width)
            turned = jnp.dot(turn, x, preferred_element_type=jnp.float32)
            left_ref[b, :width] = x.T
            left_ref[b, width:] = turned.astype(jnp.bfloat16).T

    for b in range(bins):
        y = other_ref[0, :, b].reshape(depth, width)
        both = jnp.dot(left_ref[b], y, preferred_element_type=jnp.float32) * scale
        out_ref[0, b] = both.reshape(2, width, width)


def on_device(n_chan, n_seg, spectra, plan, assignment):
    bin_count, win_count, _, width = spectra.shape
    bins, rows = bin_count // n_seg, 2 * win_count
    rounds = plan.shape[0]
    scale = 1.0 / math.sqrt(win_count * n_seg)
    chan = lax.axis_index("chan")
    slots = (assignment - chan * width).reshape(1, width)
    hops = n_chan // 2
    gathered = pl.pallas_call(
        functools.partial(gather_kernel, n_chan, n_seg),
        out_shape=jax.ShapeDtypeStruct((n_chan, n_seg, bins, rows, width), jnp.bfloat16),
        in_specs=[pl.BlockSpec(memory_space=pltpu.VMEM)] * 2,
        out_specs=pl.BlockSpec(memory_space=pl.ANY),
        scratch_shapes=[
            pltpu.VMEM((n_seg, bins, rows, width), jnp.bfloat16),
            pltpu.SemaphoreType.DMA,
            pltpu.SemaphoreType.DMA((n_seg,)),
            pltpu.SemaphoreType.DMA((n_seg,)),
            pltpu.SemaphoreType.DMA((2, hops, n_seg)),
            pltpu.SemaphoreType.DMA((2, hops, n_seg)),
        ],
        compiler_params=pltpu.CompilerParams(collective_id=0, has_side_effects=True),
        name="gather_blocks",
    )(slots, spectra.reshape(bin_count, rows, width))

    partner = lax.dynamic_index_in_dim(plan, chan, 1, keepdims=False)
    held = (ring_place(chan, n_chan) - ring_place(partner, n_chan)) % n_chan
    block = (1, n_seg, bins, rows, width)
    return pl.pallas_call(
        functools.partial(cross_kernel, scale),
        grid_spec=pltpu.PrefetchScalarGridSpec(
            num_scalar_prefetch=1,
            grid=(rounds,),
            in_specs=[
                pl.BlockSpec(block, lambda r, held: (0, 0, 0, 0, 0)),
                pl.BlockSpec(block, lambda r, held: (held[r], 0, 0, 0, 0)),
            ],
            out_specs=pl.BlockSpec((1, bins, 2, width, width), lambda r, held: (r, 0, 0, 0, 0)),
            scratch_shapes=[pltpu.VMEM((bins, 2 * width, n_seg * rows), jnp.bfloat16)],
        ),
        out_shape=jax.ShapeDtypeStruct((rounds, bins, 2, width, width), jnp.float32),
        name="cross_products",
    )(held.astype(jnp.int32), gathered, gathered)


def solution(mesh):
    in_specs = (P(None, "seg", None, "chan"), P(), P("chan"))
    out_specs = P(None, "seg", None, "chan", None)
    return jax.shard_map(
        functools.partial(on_device, mesh.shape["chan"], mesh.shape["seg"]),
        mesh=mesh, in_specs=in_specs, out_specs=out_specs, check_vma=False,
    )
```

time: 282 us -> 55.1 us (0.20)
  waiting for transfers between devices: 173 us -> 0 us
  Pallas kernels: 0 us -> 53 us
  local copies, waits for them, and re-layouts: 32.6 us -> 0.19 us
  other arithmetic: 30.1 us -> 1.72 us
  starting transfers between devices: 22.5 us -> 0 us
  between operations: 13.6 us -> 0.01 us
  matrix products: 9.46 us -> 0 us
    unnamed x2 -> x0, waiting for transfers between devices: 125 us -> none
    pallas_call x0 -> x2, Pallas kernels: none -> 53 us  [the longest x1 46.7 us: on_device(): pl.pallas_call(functools.partial(gather_kernel, n_chan, n_seg), out_shape...]
    all_to_all x5 -> x0, waiting for transfers between devices: 48 us -> none  [the longest x4 33.5 us: on_device(): lax.all_to_all(outgoing, 'chan', split_axis=0, concat_axis=0, tiled=True)]
    all_to_all x5 -> x0, starting transfers between devices: 22.3 us -> none  [the longest x4 15 us: on_device(): lax.all_to_all(outgoing, 'chan', split_axis=0, concat_axis=0, tiled=True)]
    unnamed x15 -> x2, local copies, waits for them, and re-layouts: 19 us -> 0.01 us
    another operation x5 -> x0, other arithmetic: 17.5 us -> none  [the longest x4 11.9 us: cross_block(): return jnp.stack([real_part, imag_part], axis=1)]
    dot_general x4 -> x0, matrix products: 9.46 us -> none  [cross_block(): jnp.einsum('fwa,fwb->fab', own_rows, other_rows, preferred_element_type=j...]
    gather x8 -> x0, local copies, waits for them, and re-layouts: 8.61 us -> none  [the longest x4 6.29 us: on_device(): ordered = jnp.take(spectra, local_slots, axis=3)]
  transfers between devices with their start and end apart: 6 -> 0, of which waited for: 6 -> 0; matrix products, arithmetic and copies ran while one was open for 9% -> 0% of each run, Pallas kernels for 0% -> 0%
where the time goes in v1:
time: 55.1 us; the launch traced here: 54.9 us
  Pallas kernels  53 us (96%)
  other arithmetic  1.72 us (3%)
    pallas_call x1, Pallas kernels, on_device(): pl.pallas_call(functools.partial(gather_kernel, n_chan, n_seg), out_shape...  46.7 us
    pallas_call x1, Pallas kernels, on_device(): pl.pallas_call(functools.partial(cross_kernel, scale), grid_spec=pltpu.Pr...  6.26 us
    reshape x1, other arithmetic, on_device(): slots = (assignment - chan * width).reshape(1, width)  1.18 us

profile of v1, /device:TPU:0, one launch (start us, length us, event | category | flops | bytes accessed | tf_op | source)
XLA Modules:
  0.0 54.9 jit_solution(4178164624220342756)
XLA Ops:
  0.0 0.0 copy-start
  0.0 1.2 %subtract_bitcast_fusion.slots_ref = s32[1,128]{1,0:T(1,128)} fusion(s32[128]{0:T(128)} %param.5, s32[]{:T(128)S(6)} %mul.19), kind=kLoop, calls=%fused_computation.12 | loop fusion | flops 128 | bytes 1028 | tf_op jit(solution)/shard_map/reshape | solution.py:148
  1.2 0.0 copy-done
  1.2 0.2 dynamic-slice_reduce_fusion
  1.4 0.5 and_select_fusion.held_ref
  1.9 46.7 %gather_blocks.1.own_ref.other_ref = bf16[8,4,8,64,128]{4,3,2,1,0:T(8,128)(2,1)} custom-call(s32[1,128]{1,0:T(1,128)} %subtract_bitcast_fusion.slots_ref, bf16[32,64,128]{2,1,0:T(8,128)(2,1)} %bitcast.3), custom_call_target="tpu_custom_call" | custom-call | tf_op jit(solution)/shard_map/gather_blocks/pallas_call | solution.py:150
  48.6 6.3 %cross_products.1 = f32[4,8,2,128,128]{4,3,2,1,0:T(8,128)} custom-call(s32[4]{0:T(128)} %and_select_fusion.held_ref, bf16[8,4,8,64,128]{4,3,2,1,0:T(8,128)(2,1)} %gather_blocks.1.own_ref.other_ref, bf16[8,4,8,64,128]{4,3,2,1,0:T(8,128)(2,1)} %gather_blocks.1.own_ref.other_ref), custom_call_target="tpu_custom_call" | custom-call | tf_op jit(solution)/shard_map/cross_products/pallas_call | solution.py:170
Async XLA Ops:
  0.0 1.2 %copy-start = (s32[4,8]{1,0:T(4,128)S(1)}, s32[4,8]{1,0:T(4,128)}, u32[]{:S(2)}) copy-start(s32[4,8]{1,0:T(4,128)} %param.4) | copy-start | bytes 388

commit v2 on v1

v2 whole, which is shorter than its diff:
```python
import functools
import math

import jax
import jax.numpy as jnp
from jax import lax
from jax.experimental import pallas as pl
from jax.experimental.pallas import tpu as pltpu
from jax.sharding import PartitionSpec as P

MESH = pl.DeviceIdType.MESH


def ring_place(chan, n_chan):
    z, x = chan // 2, chan % 2
    return z + x * (n_chan - 1 - 2 * z)


def ring_chan(place, n_chan):
    x = place // (n_chan // 2)
    z = place + x * (n_chan - 1 - 2 * place)
    return 2 * z + x


def seg_peer(seg, step, n_seg):
    pair = (seg // 2 + step // 2) % (n_seg // 2)
    return 2 * pair + (seg % 2 + step) % 2


def cross_ring_kernel(
    n_chan, n_seg, scale, assign_ref, x_ref, out_ref,
    entry_ref, sorted_ref, block_ref, left_ref, stage_ref,
    entry_sem, stage_sem, seg_send, seg_recv, ring_send, ring_recv,
):
    chan, seg = lax.axis_index("chan"), lax.axis_index("seg")
    place = ring_place(chan, n_chan)
    sides = (
        ring_chan((place + 1) % n_chan, n_chan),
        ring_chan((place + n_chan - 1) % n_chan, n_chan),
    )
    peers = [seg_peer(seg, step, n_seg) for step in range(n_seg)]
    _, bins, rows, width = sorted_ref.shape
    depth = n_seg * rows
    hops = n_chan // 2
    turns = n_seg
    turn_bins = bins // turns

    barrier = pltpu.get_barrier_semaphore()
    for side in sides:
        pl.semaphore_signal(barrier, inc=1, device_id=(side, seg), device_id_type=MESH)
    for peer in peers[1:]:
        pl.semaphore_signal(barrier, inc=1, device_id=(chan, peer), device_id_type=MESH)

    order = [0] + list(range(2, n_seg)) + [1]
    entry = {
        step: pltpu.make_async_copy(
            x_ref.at[pl.ds(peers[step] * bins, bins)], entry_ref.at[step], entry_sem.at[step]
        )
        for step in order
    }
    for step in order:
        entry[step].start()

    column = lax.broadcasted_iota(jnp.int32, (width, width), 0) + chan * width
    pick = (column == assign_ref[...]).astype(jnp.float32).astype(jnp.bfloat16)

    def sort_part(step):
        entry[step].wait()
        part = entry_ref[step].reshape(bins * rows, width)
        part = jnp.dot(part, pick, preferred_element_type=jnp.float32)
        return part.astype(jnp.bfloat16).reshape(bins, rows, width)

    def ring_copy(way, hop, part):
        held = (n_chan - hop) % n_chan if way else hop
        lands = n_chan - hop - 1 if way else hop + 1
        return pltpu.make_async_remote_copy(
            src_ref=block_ref.at[held, part],
            dst_ref=block_ref.at[lands, part],
            send_sem=ring_send.at[way, hop, part],
            recv_sem=ring_recv.at[way, hop, part],
            device_id=(sides[way], seg),
            device_id_type=MESH,
        )

    def goes(way, hop, part):
        return hop < hops - 1 or (part >= n_seg // 2) == bool(way)

    ring = {
        (way, hop, part): ring_copy(way, hop, part)
        for hop in range(hops)
        for part in range(n_seg)
        for way in range(2)
        if goes(way, hop, part)
    }
    swap = {
        step: pltpu.make_async_remote_copy(
            src_ref=sorted_ref.at[step],
            dst_ref=block_ref.at[0, step],
            send_sem=seg_send.at[step],
            recv_sem=seg_recv.at[step],
            device_id=(chan, peers[step]),
            device_id_type=MESH,
        )
        for step in range(1, n_seg)
    }

    def make_left():
        row = lax.broadcasted_iota(jnp.int32, (depth, depth), 0)
        col = lax.broadcasted_iota(jnp.int32, (depth, depth), 1)
        up = ((row % 2 == 0) & (col == row + 1)).astype(jnp.float32)
        down = ((row % 2 == 1) & (col == row - 1)).astype(jnp.float32)
        turn = (up - down).astype(jnp.bfloat16)
        for b in range(bins):
            x = block_ref[0, :, b].reshape(depth, width)
            turned = jnp.dot(turn, x, preferred_element_type=jnp.float32)
            left_ref[b, :width] = x.T
            left_ref[b, width:] = turned.astype(jnp.bfloat16).T

    leaving = {}
    stages = stage_ref.shape[0]

    def product(slot, turn):
        number = 2 * slot - 2 if slot <= hops else 2 * (n_chan - slot) - 1
        stage = number % stages
        if (stage, turn) in leaving:
            leaving[stage, turn].wait()
        for b in range(turn * turn_bins, (turn + 1) * turn_bins):
            y = block_ref[slot, :, b].reshape(depth, width)
            both = jnp.dot(left_ref[b], y, preferred_element_type=jnp.float32) * scale
            stage_ref[stage, b] = both.reshape(2, width, width)
        some = pl.ds(turn * turn_bins, turn_bins)
        leaving[stage, turn] = pltpu.make_async_copy(
            stage_ref.at[stage, some], out_ref.at[slot - 1, some], stage_sem.at[stage, turn]
        )
        leaving[stage, turn].start()

    block_ref[0, 0] = sort_part(0)
    pl.semaphore_wait(barrier, 1 + n_seg)
    ring[0, 0, 0].start()
    ring[1, 0, 0].start()
    for step in order[1:]:
        sorted_ref[step] = sort_part(step)
        swap[step].start()

    for hop in range(hops):
        for part in range(n_seg):
            if hop == 0 and part > 0:
                swap[part].wait_recv()
            for way in range(2):
                if hop > 0 and (way, hop - 1, part) in ring:
                    ring[way, hop - 1, part].wait_recv()
                if (way, hop, part) in ring and (hop, part) != (0, 0):
                    ring[way, hop, part].start()
            if hop > 1:
                product(hop - 1, part)
                product(n_chan - hop + 1, part)
        if hop == 0:
            make_left()
    for turn in range(turns):
        if hops > 1:
            product(hops - 1, turn)
            product(n_chan - hops + 1, turn)
    for part in range(n_seg):
        for way in range(2):
            if (way, hops - 1, part) in ring:
                ring[way, hops - 1, part].wait_recv()
    for turn in range(turns):
        product(hops, turn)
    for step in range(1, n_seg):
        swap[step].wait_send()
    for copy in ring.values():
        copy.wait_send()
    for copy in leaving.values():
        copy.wait()


def choose_kernel(n_chan, plan_ref, product_ref, out_ref, sem):
    chan = lax.axis_index("chan")
    place = ring_place(chan, n_chan)
    copies = []
    for r in range(out_ref.shape[0]):
        away = place + n_chan - ring_place(plan_ref[r, chan], n_chan)
        slot = lax.rem(away, n_chan) - 1
        copies.append(pltpu.make_async_copy(product_ref.at[slot], out_ref.at[r], sem.at[r]))
        copies[-1].start()
    for copy in copies:
        copy.wait()


def on_device(n_chan, n_seg, spectra, plan, assignment):
    bin_count, win_count, _, width = spectra.shape
    bins, rows = bin_count // n_seg, 2 * win_count
    rounds = plan.shape[0]
    scale = 1.0 / math.sqrt(win_count * n_seg)
    hops = n_chan // 2
    part = (n_seg, bins, rows, width)
    spent = 2 * n_chan * n_seg * bins * rows * width
    products = pl.pallas_call(
        functools.partial(cross_ring_kernel, n_chan, n_seg, scale),
        out_shape=jax.ShapeDtypeStruct((n_chan - 1, bins, 2, width, width), jnp.float32),
        in_specs=[pl.BlockSpec(memory_space=pltpu.VMEM), pl.BlockSpec(memory_space=pl.ANY)],
        out_specs=pl.BlockSpec(memory_space=pl.ANY),
        scratch_shapes=[
            pltpu.VMEM(part, jnp.bfloat16),
            pltpu.VMEM(part, jnp.bfloat16),
            pltpu.VMEM((n_chan,) + part, jnp.bfloat16),
            pltpu.VMEM((bins, 2 * width, n_seg * rows), jnp.bfloat16),
            pltpu.VMEM((4, bins, 2, width, width), jnp.float32),
            pltpu.SemaphoreType.DMA((n_seg,)),
            pltpu.SemaphoreType.DMA((4, n_seg)),
            pltpu.SemaphoreType.DMA((n_seg,)),
            pltpu.SemaphoreType.DMA((n_seg,)),
            pltpu.SemaphoreType.DMA((2, hops, n_seg)),
            pltpu.SemaphoreType.DMA((2, hops, n_seg)),
        ],
        compiler_params=pltpu.CompilerParams(
            collective_id=0, has_side_effects=True, vmem_limit_bytes=spent + (14 << 20)
        ),
        name="cross_ring",
    )(assignment.reshape(1, width), spectra.reshape(bin_count, rows, width))

    return pl.pallas_call(
        functools.partial(choose_kernel, n_chan),
        out_shape=jax.ShapeDtypeStruct((rounds, bins, 2, width, width), jnp.float32),
        in_specs=[pl.BlockSpec(memory_space=pltpu.SMEM), pl.BlockSpec(memory_space=pl.ANY)],
        out_specs=pl.BlockSpec(memory_space=pl.ANY),
        scratch_shapes=[pltpu.SemaphoreType.DMA((rounds,))],
        compiler_params=pltpu.CompilerParams(vmem_limit_bytes=4 << 20),
        name="choose_products",
    )(plan, products)


def solution(mesh):
    in_specs = (P(None, "seg", None, "chan"), P(), P("chan"))
    out_specs = P(None, "seg", None, "chan", None)
    return jax.shard_map(
        functools.partial(on_device, mesh.shape["chan"], mesh.shape["seg"]),
        mesh=mesh, in_specs=in_specs, out_specs=out_specs, check_vma=False,
    )
```

time: 55.1 us -> 51.2 us (0.929)
  Pallas kernels: 53 us -> 49.3 us
  other arithmetic: 1.72 us -> 0 us
  local copies, waits for them, and re-layouts: 0.19 us -> 1.71 us
    pallas_call x2, Pallas kernels: 53 us -> 49.3 us  [the longest x1 46.7 us: on_device(): pl.pallas_call(functools.partial(cross_ring_kernel, n_chan, n_seg, scale)...]
    unnamed x2 -> x6, local copies, waits for them, and re-layouts: 0.01 us -> 1.71 us
    reshape x1 -> x0, other arithmetic: 1.18 us -> none  [on_device(): slots = (assignment - chan * width).reshape(1, width)]
where the time goes in v2:
time: 51.2 us; the launch traced here: 51.1 us
  Pallas kernels  49.3 us (96%)
  local copies, waits for them, and re-layouts  1.71 us (3%)
    pallas_call x1, Pallas kernels, on_device(): pl.pallas_call(functools.partial(cross_ring_kernel, n_chan, n_seg, scale)...  46.7 us
    pallas_call x1, Pallas kernels, on_device(): pl.pallas_call(functools.partial(choose_kernel, n_chan), out_shape=jax.Sh...  2.64 us
    unnamed x6, local copies, waits for them, and re-layouts  1.71 us

profile of v2, /device:TPU:0, one launch (start us, length us, event | category | flops | bytes accessed | tf_op | source)
XLA Modules:
  0.0 51.1 jit_solution(3199283358927165680)
XLA Ops:
  0.0 0.0 copy-start.1
  0.0 0.0 copy-start
  0.0 1.1 %copy-done = bf16[32,32,2,128]{3,2,1,0:T(2,128)(2,1)S(1)} copy-done((bf16[32,32,2,128]{3,2,1,0:T(2,128)(2,1)S(1)}, bf16[32,32,2,128]{3,2,1,0:T(2,128)(2,1)}, u32[]{:S(2)}) %copy-start) | copy-done | bytes 524312
  1.1 0.0 copy-start.2
  1.1 0.7 %copy-done.2 = s32[128]{0:T(128)S(1)} copy-done((s32[128]{0:T(128)S(1)}, s32[128]{0:T(128)}, u32[]{:S(2)}) %copy-start.2) | copy-done | bytes 536
  1.7 46.7 %cross_ring.1.product_ref = f32[7,8,2,128,128]{4,3,2,1,0:T(8,128)S(1)} custom-call(s32[1,128]{1,0:T(1,128)S(1)} %bitcast.3, bf16[32,64,128]{2,1,0:T(8,128)(2,1)S(1)} %bitcast.2), custom_call_target="tpu_custom_call" | custom-call | tf_op jit(solution)/shard_map/cross_ring/pallas_call | solution.py:198
  48.4 0.0 copy-done.1
  48.4 2.6 %choose_products.1 = f32[4,8,2,128,128]{4,3,2,1,0:T(8,128)} custom-call(s32[4,8]{1,0:T(4,128)S(1)} %copy-done.1, f32[7,8,2,128,128]{4,3,2,1,0:T(8,128)S(1)} %cross_ring.1.product_ref), custom_call_target="tpu_custom_call" | custom-call | tf_op jit(solution)/shard_map/choose_products/pallas_call | solution.py:222
Async XLA Ops:
  0.0 48.4 %copy-start.1 = (s32[4,8]{1,0:T(4,128)S(1)}, s32[4,8]{1,0:T(4,128)}, u32[]{:S(2)}) copy-start(s32[4,8]{1,0:T(4,128)} %plan_ref.1) | copy-start | bytes 388
  0.0 1.1 %copy-start = (bf16[32,32,2,128]{3,2,1,0:T(2,128)(2,1)S(1)}, bf16[32,32,2,128]{3,2,1,0:T(2,128)(2,1)}, u32[]{:S(2)}) copy-start(bf16[32,32,2,128]{3,2,1,0:T(2,128)(2,1)} %param.3) | copy-start | bytes 1572868
  1.1 0.7 %copy-start.2 = (s32[128]{0:T(128)S(1)}, s32[128]{0:T(128)}, u32[]{:S(2)}) copy-start(s32[128]{0:T(128)} %param.5) | copy-start | bytes 1540

commit v3 on v2

--- a/solution.py
+++ b/solution.py
@@ -28,8 +28,8 @@
 
 
 def cross_ring_kernel(
-    n_chan, n_seg, scale, assign_ref, x_ref, out_ref,
-    entry_ref, sorted_ref, block_ref, left_ref, stage_ref,
+    n_chan, n_seg, scale, slots_ref, x_ref, out_ref,
+    assign_ref, assign_sem, entry_ref, sorted_ref, block_ref, left_ref, stage_ref,
     entry_sem, stage_sem, seg_send, seg_recv, ring_send, ring_recv,
 ):
     chan, seg = lax.axis_index("chan"), lax.axis_index("seg")
@@ -58,8 +58,11 @@
         )
         for step in order
     }
+    slots = pltpu.make_async_copy(slots_ref, assign_ref, assign_sem)
+    slots.start()
     for step in order:
         entry[step].start()
+    slots.wait()
 
     column = lax.broadcasted_iota(jnp.int32, (width, width), 0) + chan * width
     pick = (column == assign_ref[...]).astype(jnp.float32).astype(jnp.bfloat16)
@@ -181,8 +184,9 @@
     for r in range(out_ref.shape[0]):
         away = place + n_chan - ring_place(plan_ref[r, chan], n_chan)
         slot = lax.rem(away, n_chan) - 1
-        copies.append(pltpu.make_async_copy(product_ref.at[slot], out_ref.at[r], sem.at[r]))
-        copies[-1].start()
+        for b in range(out_ref.shape[1]):
+            copies.append(pltpu.make_async_copy(product_ref.at[slot, b], out_ref.at[r, b], sem.at[r, b]))
+            copies[-1].start()
     for copy in copies:
         copy.wait()
 
@@ -198,9 +202,11 @@
     products = pl.pallas_call(
         functools.partial(cross_ring_kernel, n_chan, n_seg, scale),
         out_shape=jax.ShapeDtypeStruct((n_chan - 1, bins, 2, width, width), jnp.float32),
-        in_specs=[pl.BlockSpec(memory_space=pltpu.VMEM), pl.BlockSpec(memory_space=pl.ANY)],
+        in_specs=[pl.BlockSpec(memory_space=pltpu.HBM)] * 2,
         out_specs=pl.BlockSpec(memory_space=pl.ANY),
         scratch_shapes=[
+            pltpu.VMEM((1, width), jnp.int32),
+            pltpu.SemaphoreType.DMA,
             pltpu.VMEM(part, jnp.bfloat16),
             pltpu.VMEM(part, jnp.bfloat16),
             pltpu.VMEM((n_chan,) + part, jnp.bfloat16),
@@ -217,14 +223,17 @@
             collective_id=0, has_side_effects=True, vmem_limit_bytes=spent + (14 << 20)
         ),
         name="cross_ring",
-    )(assignment.reshape(1, width), spectra.reshape(bin_count, rows, width))
+    )(
+        pltpu.with_memory_space_constraint(assignment.reshape(1, width), pltpu.HBM),
+        pltpu.with_memory_space_constraint(spectra.reshape(bin_count, rows, width), pltpu.HBM),
+    )
 
     return pl.pallas_call(
         functools.partial(choose_kernel, n_chan),
         out_shape=jax.ShapeDtypeStruct((rounds, bins, 2, width, width), jnp.float32),
         in_specs=[pl.BlockSpec(memory_space=pltpu.SMEM), pl.BlockSpec(memory_space=pl.ANY)],
         out_specs=pl.BlockSpec(memory_space=pl.ANY),
-        scratch_shapes=[pltpu.SemaphoreType.DMA((rounds,))],
+        scratch_shapes=[pltpu.SemaphoreType.DMA((rounds, bins))],
         compiler_params=pltpu.CompilerParams(vmem_limit_bytes=4 << 20),
         name="choose_products",
     )(plan, products)

time: 51.2 us -> 49.7 us (0.971)
  local copies, waits for them, and re-layouts: 1.71 us -> 0.01 us
    unnamed x6 -> x2, local copies, waits for them, and re-layouts: 1.71 us -> 0.01 us
where the time goes in v3:
time: 49.7 us; the launch traced here: 49.6 us
  Pallas kernels  49.6 us (100%)
    pallas_call x1, Pallas kernels, on_device(): pl.pallas_call(functools.partial(cross_ring_kernel, n_chan, n_seg, scale)...  46.7 us
    pallas_call x1, Pallas kernels, on_device(): pl.pallas_call(functools.partial(choose_kernel, n_chan), out_shape=jax.Sh...  2.86 us

profile of v3, /device:TPU:0, one launch (start us, length us, event | category | flops | bytes accessed | tf_op | source)
XLA Modules:
  0.0 49.6 jit_solution(13179450126306111531)
XLA Ops:
  0.0 0.0 copy-start
  0.0 46.7 %cross_ring.1.product_ref = f32[7,8,2,128,128]{4,3,2,1,0:T(8,128)S(1)} custom-call(s32[1,128]{1,0:T(1,128)} %bitcast.3, bf16[32,64,128]{2,1,0:T(8,128)(2,1)} %bitcast.2), custom_call_target="tpu_custom_call" | custom-call | tf_op jit(solution)/shard_map/cross_ring/pallas_call | solution.py:202
  46.7 0.0 copy-done
  46.7 2.9 %choose_products.1 = f32[4,8,2,128,128]{4,3,2,1,0:T(8,128)} custom-call(s32[4,8]{1,0:T(4,128)S(1)} %copy-done, f32[7,8,2,128,128]{4,3,2,1,0:T(8,128)S(1)} %cross_ring.1.product_ref), custom_call_target="tpu_custom_call" | custom-call | tf_op jit(solution)/shard_map/choose_products/pallas_call | solution.py:231
Async XLA Ops:
  0.0 46.7 %copy-start = (s32[4,8]{1,0:T(4,128)S(1)}, s32[4,8]{1,0:T(4,128)}, u32[]{:S(2)}) copy-start(s32[4,8]{1,0:T(4,128)} %plan_ref.1) | copy-start | bytes 388

commit v4 on v0

v4 whole, which is shorter than its diff:
```python
import functools
import math

import jax
import jax.numpy as jnp
from jax import lax
from jax.experimental import pallas as pl
from jax.experimental.pallas import tpu as pltpu
from jax.sharding import PartitionSpec as P

MESH = pl.DeviceIdType.MESH


def seg_peer(seg, step, n_seg):
    pair = (seg // 2 + step // 2) % (n_seg // 2)
    return 2 * pair + (seg % 2 + step) % 2


def column_kernel(
    n_chan, n_seg, rounds, slots_ref, plan_ref, x_ref, out_ref, left_out_ref,
    assign_ref, entry_ref, sorted_ref, own_ref, left_ref, keep_ref, give_ref,
    assign_sem, entry_sem, left_sem, keep_sem, own_send, own_recv, mate_send, mate_recv,
    z_send, z_recv, x_send, x_recv, *gathered,
):
    chan, seg = lax.axis_index("chan"), lax.axis_index("seg")
    layers = n_chan // 2
    z, x = chan // 2, chan % 2
    mate = chan + 1 - 2 * x
    peers = [seg_peer(seg, step, n_seg) for step in range(n_seg)]
    _, bins, rows, width = sorted_ref.shape
    depth = n_seg * rows
    half = bins // 2
    subs = 2
    some = half // subs
    chunks = n_seg * subs

    def remote(src, dst, send, recv, to):
        return pltpu.make_async_remote_copy(
            src_ref=src, dst_ref=dst, send_sem=send, recv_sem=recv, device_id=to, device_id_type=MESH
        )

    barrier = pltpu.get_barrier_semaphore()

    def greet(to):
        pl.semaphore_signal(barrier, inc=1, device_id=to, device_id_type=MESH)

    greet((mate, seg))
    for peer in peers[1:]:
        greet((chan, peer))
        greet((mate, peer))

    @pl.when(z > 0)
    def _():
        greet((chan - 2, seg))

    @pl.when(z < layers - 1)
    def _():
        greet((chan + 2, seg))

    order = [0, 1] + list(range(2, n_seg))
    entry = {
        step: pltpu.make_async_copy(
            x_ref.at[pl.ds(peers[step] * bins, bins)], entry_ref.at[step], entry_sem.at[step]
        )
        for step in order
    }
    slots = pltpu.make_async_copy(slots_ref, assign_ref, assign_sem)
    slots.start()
    for step in order:
        entry[step].start()
    slots.wait()

    column = lax.broadcasted_iota(jnp.int32, (width, width), 0) + chan * width
    pick = (column == assign_ref[...]).astype(jnp.float32).astype(jnp.bfloat16)

    def sort_part(step):
        entry[step].wait()
        part = entry_ref[step].reshape(bins * rows, width)
        part = jnp.dot(part, pick, preferred_element_type=jnp.float32)
        return part.astype(jnp.bfloat16).reshape(bins, rows, width)

    def to_own(step):
        return remote(
            sorted_ref.at[step], own_ref.at[step], own_send.at[step], own_recv.at[step],
            (chan, peers[step]),
        )

    def to_mate(step, sub):
        source = own_ref if step == 0 else sorted_ref
        return remote(
            source.at[step, pl.ds((1 - x) * half + sub * some, some)],
            gathered[step * subs + sub].at[chan],
            mate_send.at[step, sub], mate_recv.at[step, sub], (mate, peers[step]),
        )

    def from_mate(step, sub):
        into = gathered[step * subs + sub].at[mate]
        return remote(into, into, mate_send.at[step, sub], mate_recv.at[step, sub], (mate, seg))

    def z_pass(way, chunk, far):
        layer = z + far if way else z - far
        pack = gathered[chunk].at[pl.ds(2 * layer, 2)]
        to = chan - 2 if way else chan + 2
        return remote(pack, pack, z_send.at[way, chunk, far], z_recv.at[way, chunk, far], (to, seg))

    def z_arrival(way, chunk, far):
        layer = z + 1 + far if way else z - 1 - far
        pack = gathered[chunk].at[pl.ds(2 * layer, 2)]
        to = chan + 2 if way else chan - 2
        return remote(pack, pack, z_send.at[way, chunk, far], z_recv.at[way, chunk, far], (to, seg))

    def passes(way, far):
        if way:
            return (z <= layers - 1 - far) & (z >= 1)
        return (z >= far) & (z <= layers - 2)

    def arrives(way, far):
        return z <= layers - 2 - far if way else z >= far + 1

    def place_of(chunk):
        return chunk // subs, chunk % subs

    def x_pass(chunk):
        part, sub = place_of(chunk)
        return remote(
            give_ref.at[chunk], out_ref.at[x, part, sub], x_send.at[chunk], x_recv.at[chunk], (mate, seg)
        )

    def x_arrival(chunk):
        part, sub = place_of(chunk)
        return remote(
            give_ref.at[chunk], out_ref.at[1 - x, part, sub], x_send.at[chunk], x_recv.at[chunk], (mate, seg)
        )

    def keep(chunk):
        part, sub = place_of(chunk)
        return pltpu.make_async_copy(keep_ref.at[chunk], out_ref.at[x, part, sub], keep_sem.at[chunk])

    own_ref[0] = sort_part(0)
    pl.semaphore_wait(barrier, 2 * n_seg - 1 + (z + layers - 1) // layers + (2 * layers - 2 - z) // layers)
    for step in order:
        if step > 0:
            sorted_ref[step] = sort_part(step)
        for sub in range(subs):
            to_mate(step, sub).start()
        if step > 0:
            to_own(step).start()

    def begin(chunk):
        part, sub = place_of(chunk)
        if sub == 0 and part > 0:
            to_own(part).wait_recv()
        gathered[chunk][chan] = own_ref[part, pl.ds(x * half + sub * some, some)]
        from_mate(part, sub).wait_recv()

    def await_layer(way, chunk, far):
        @pl.when(arrives(way, far))
        def _():
            z_arrival(way, chunk, far).wait_recv()

    def send_layer(way, chunk, far):
        @pl.when(passes(way, far))
        def _():
            z_pass(way, chunk, far).start()

    def choose(chunk):
        for r in range(rounds):
            give_ref[chunk, r] = gathered[chunk][plan_ref[r, mate]]
        x_pass(chunk).start()
        for r in range(rounds):
            keep_ref[chunk, r] = gathered[chunk][plan_ref[r, chan]]
        keep(chunk).start()

    def make_left():
        row = lax.broadcasted_iota(jnp.int32, (depth, depth), 0)
        col = lax.broadcasted_iota(jnp.int32, (depth, depth), 1)
        up = ((row % 2 == 0) & (col == row + 1)).astype(jnp.float32)
        down = ((row % 2 == 1) & (col == row - 1)).astype(jnp.float32)
        turn = (up - down).astype(jnp.bfloat16)
        for b in range(bins):
            own = own_ref[:, b].reshape(depth, width)
            turned = jnp.dot(turn, own, preferred_element_type=jnp.float32)
            left_ref[b, :width] = own.T
            left_ref[b, width:] = turned.astype(jnp.bfloat16).T

    left = pltpu.make_async_copy(left_ref, left_out_ref, left_sem)
    for time in range(chunks + layers - 1):
        for far in range(layers - 1):
            chunk = time - far
            if 0 <= chunk < chunks:
                if far == 0:
                    begin(chunk)
                for way in range(2):
                    if far > 0:
                        await_layer(way, chunk, far - 1)
                    send_layer(way, chunk, far)
        if time == chunks - 1:
            make_left()
            left.start()
        last = time - (layers - 1)
        if last >= 0:
            for way in range(2):
                await_layer(way, last, layers - 2)
            choose(last)

    left.wait()
    for step in range(n_seg):
        if step > 0:
            to_own(step).wait_send()
        for sub in range(subs):
            to_mate(step, sub).wait_send()
    for chunk in range(chunks):
        for far in range(layers - 1):
            for way in range(2):
                @pl.when(passes(way, far))
                def _():
                    z_pass(way, chunk, far).wait_send()
    for chunk in range(chunks):
        keep(chunk).wait()
        x_pass(chunk).wait_send()
        x_arrival(chunk).wait_recv()


def cross_kernel(scale, left_ref, other_ref, out_ref):
    _, parts, subs, _, some, rows, width = other_ref.shape
    for b in range(subs * some):
        y = other_ref[0, :, b // some, 0, b % some].reshape(parts * rows, width)
        both = jnp.dot(left_ref[b], y, preferred_element_type=jnp.float32) * scale
        out_ref[0, b] = both.reshape(2, width, width)


def on_device(n_chan, n_seg, spectra, plan, assignment):
    bin_count, win_count, _, width = spectra.shape
    bins, rows = bin_count // n_seg, 2 * win_count
    rounds = plan.shape[0]
    scale = 1.0 / math.sqrt(win_count * n_seg)
    depth = n_seg * rows
    layers = n_chan // 2
    half, subs = bins // 2, 2
    some, chunks = half // subs, n_seg * subs
    part = (n_seg, bins, rows, width)
    chosen = (chunks, rounds, some, rows, width)
    spent = n_chan * n_seg * bins * rows * width
    others, lefts = pl.pallas_call(
        functools.partial(column_kernel, n_chan, n_seg, rounds),
        out_shape=(
            jax.ShapeDtypeStruct((2, n_seg, subs, rounds, some, rows, width), jnp.bfloat16),
            jax.ShapeDtypeStruct((bins, 2 * width, depth), jnp.bfloat16),
        ),
        in_specs=[
            pl.BlockSpec(memory_space=pltpu.HBM),
            pl.BlockSpec(memory_space=pltpu.SMEM),
            pl.BlockSpec(memory_space=pltpu.HBM),
        ],
        out_specs=[pl.BlockSpec(memory_space=pl.ANY)] * 2,
        scratch_shapes=[
            pltpu.VMEM((1, width), jnp.int32),
            pltpu.VMEM(part, jnp.bfloat16),
            pltpu.VMEM(part, jnp.bfloat16),
            pltpu.VMEM(part, jnp.bfloat16),
            pltpu.VMEM((bins, 2 * width, depth), jnp.bfloat16),
            pltpu.VMEM(chosen, jnp.bfloat16),
            pltpu.VMEM(chosen, jnp.bfloat16),
            pltpu.SemaphoreType.DMA,
            pltpu.SemaphoreType.DMA((n_seg,)),
            pltpu.SemaphoreType.DMA,
            pltpu.SemaphoreType.DMA((chunks,)),
            pltpu.SemaphoreType.DMA((n_seg,)),
            pltpu.SemaphoreType.DMA((n_seg,)),
            pltpu.SemaphoreType.DMA((n_seg, subs)),
            pltpu.SemaphoreType.DMA((n_seg, subs)),
            pltpu.SemaphoreType.DMA((2, chunks, layers - 1)),
            pltpu.SemaphoreType.DMA((2, chunks, layers - 1)),
            pltpu.SemaphoreType.DMA((chunks,)),
            pltpu.SemaphoreType.DMA((chunks,)),
        ] + [pltpu.VMEM((n_chan, some, rows, width), jnp.bfloat16)] * chunks,
        compiler_params=pltpu.CompilerParams(
            collective_id=0, has_side_effects=True, vmem_limit_bytes=spent + (16 << 20)
        ),
        name="gather_columns",
    )(
        pltpu.with_memory_space_constraint(assignment.reshape(1, width), pltpu.HBM),
        pltpu.with_memory_space_constraint(plan, pltpu.HBM),
        pltpu.with_memory_space_constraint(spectra.reshape(bin_count, rows, width), pltpu.HBM),
    )

    return pl.pallas_call(
        functools.partial(cross_kernel, scale),
        grid=(2, rounds),
        out_shape=jax.ShapeDtypeStruct((rounds, bins, 2, width, width), jnp.float32),
        in_specs=[
            pl.BlockSpec((half, 2 * width, depth), lambda h, r: (h, 0, 0)),
            pl.BlockSpec((1, n_seg, subs, 1, some, rows, width), lambda h, r: (h, 0, 0, r, 0, 0, 0)),
        ],
        out_specs=pl.BlockSpec((1, half, 2, width, width), lambda h, r: (r, h, 0, 0, 0)),
        compiler_params=pltpu.CompilerParams(vmem_limit_bytes=16 << 20),
        name="cross_products",
    )(lefts, others)


def solution(mesh):
    in_specs = (P(None, "seg", None, "chan"), P(), P("chan"))
    out_specs = P(None, "seg", None, "chan", None)
    return jax.shard_map(
        functools.partial(on_device, mesh.shape["chan"], mesh.shape["seg"]),
        mesh=mesh, in_specs=in_specs, out_specs=out_specs, check_vma=False,
    )
```

time: 282 us -> 54.9 us (0.19)
  waiting for transfers between devices: 173 us -> 0 us
  Pallas kernels: 0 us -> 54.7 us
  local copies, waits for them, and re-layouts: 32.6 us -> 0 us
  other arithmetic: 30.1 us -> 0 us
  starting transfers between devices: 22.5 us -> 0 us
  between operations: 13.6 us -> 0.01 us
  matrix products: 9.46 us -> 0 us
    unnamed x2 -> x0, waiting for transfers between devices: 125 us -> none
    pallas_call x0 -> x2, Pallas kernels: none -> 54.7 us  [the longest x1 50 us: on_device(): pl.pallas_call(functools.partial(column_kernel, n_chan, n_seg, rounds), o...]
    all_to_all x5 -> x0, waiting for transfers between devices: 48 us -> none  [the longest x4 33.5 us: on_device(): lax.all_to_all(outgoing, 'chan', split_axis=0, concat_axis=0, tiled=True)]
    all_to_all x5 -> x0, starting transfers between devices: 22.3 us -> none  [the longest x4 15 us: on_device(): lax.all_to_all(outgoing, 'chan', split_axis=0, concat_axis=0, tiled=True)]
    unnamed x15 -> x0, local copies, waits for them, and re-layouts: 19 us -> none
    another operation x5 -> x0, other arithmetic: 17.5 us -> none  [the longest x4 11.9 us: cross_block(): return jnp.stack([real_part, imag_part], axis=1)]
    dot_general x4 -> x0, matrix products: 9.46 us -> none  [cross_block(): jnp.einsum('fwa,fwb->fab', own_rows, other_rows, preferred_element_type=j...]
    gather x8 -> x0, local copies, waits for them, and re-layouts: 8.61 us -> none  [the longest x4 6.29 us: on_device(): ordered = jnp.take(spectra, local_slots, axis=3)]
  transfers between devices with their start and end apart: 6 -> 0, of which waited for: 6 -> 0; matrix products, arithmetic and copies ran while one was open for 9% -> 0% of each run, Pallas kernels for 0% -> 0%
where the time goes in v4:
time: 54.9 us; the launch traced here: 54.8 us
  Pallas kernels  54.7 us (100%)
    pallas_call x1, Pallas kernels, on_device(): pl.pallas_call(functools.partial(column_kernel, n_chan, n_seg, rounds), o...  50 us
    pallas_call x1, Pallas kernels, on_device(): pl.pallas_call(functools.partial(cross_kernel, scale), grid=(2, rounds),...  4.74 us

profile of v4, /device:TPU:0, one launch (start us, length us, event | category | flops | bytes accessed | tf_op | source)
XLA Modules:
  0.0 54.8 jit_solution(8675309041266918803)
XLA Ops:
  0.0 50.0 %gather_columns.1 = (bf16[2,4,2,4,2,64,128]{6,5,4,3,2,1,0:T(8,128)(2,1)S(1)}, bf16[8,256,256]{2,1,0:T(8,128)(2,1)S(1)}) custom-call(s32[1,128]{1,0:T(1,128)} %bitcast.3, s32[4,8]{1,0:T(4,128)} %plan_ref.1, bf16[32,64,128]{2,1,0:T(8,128)(2,1)} %bitcast.2), custom_call_target="tpu_custom_call" | custom-call | tf_op jit(solution)/shard_map/gather_columns/pallas_call | solution.py:244
  50.0 4.7 %cross_products.1 = f32[4,8,2,128,128]{4,3,2,1,0:T(8,128)} custom-call(bf16[8,256,256]{2,1,0:T(8,128)(2,1)S(1)} %get-tuple-element.7.left_ref, bf16[2,4,2,4,2,64,128]{6,5,4,3,2,1,0:T(8,128)(2,1)S(1)} %get-tuple-element.8.other_ref), custom_call_target="tpu_custom_call" | custom-call | tf_op jit(solution)/shard_map/cross_products/pallas_call | solution.py:287

commit v5 on v4

--- a/solution.py
+++ b/solution.py
@@ -109,6 +109,9 @@
         to = chan + 2 if way else chan - 2
         return remote(pack, pack, z_send.at[way, chunk, far], z_recv.at[way, chunk, far], (to, seg))
 
+    def lag(far):
+        return 1 if far > 0 else 2
+
     def passes(way, far):
         if way:
             return (z <= layers - 1 - far) & (z >= 1)
@@ -161,6 +164,9 @@
     def send_layer(way, chunk, far):
         @pl.when(passes(way, far))
         def _():
+            before = chunk - lag(far)
+            if before >= 0:
+                z_pass(way, before, far).wait_send()
             z_pass(way, chunk, far).start()
 
     def choose(chunk):
@@ -209,8 +215,8 @@
             to_own(step).wait_send()
         for sub in range(subs):
             to_mate(step, sub).wait_send()
-    for chunk in range(chunks):
-        for far in range(layers - 1):
+    for far in range(layers - 1):
+        for chunk in range(chunks - lag(far), chunks):
             for way in range(2):
                 @pl.when(passes(way, far))
                 def _():

time: 54.9 us -> 55.4 us (level)
  Pallas kernels: 54.7 us -> 55.3 us
where the time goes in v5:
time: 55.4 us; the launch traced here: 55.3 us
  Pallas kernels  55.3 us (100%)
    pallas_call x1, Pallas kernels, on_device(): pl.pallas_call(functools.partial(column_kernel, n_chan, n_seg, rounds), o...  50.5 us
    pallas_call x1, Pallas kernels, on_device(): pl.pallas_call(functools.partial(cross_kernel, scale), grid=(2, rounds),...  4.74 us

profile of v5, /device:TPU:0, one launch (start us, length us, event | category | flops | bytes accessed | tf_op | source)
XLA Modules:
  0.0 55.3 jit_solution(2895856906390849289)
XLA Ops:
  0.0 50.5 %gather_columns.1 = (bf16[2,4,2,4,2,64,128]{6,5,4,3,2,1,0:T(8,128)(2,1)S(1)}, bf16[8,256,256]{2,1,0:T(8,128)(2,1)S(1)}) custom-call(s32[1,128]{1,0:T(1,128)} %bitcast.3, s32[4,8]{1,0:T(4,128)} %plan_ref.1, bf16[32,64,128]{2,1,0:T(8,128)(2,1)} %bitcast.2), custom_call_target="tpu_custom_call" | custom-call | tf_op jit(solution)/shard_map/gather_columns/pallas_call | solution.py:250
  50.5 4.7 %cross_products.1 = f32[4,8,2,128,128]{4,3,2,1,0:T(8,128)} custom-call(bf16[8,256,256]{2,1,0:T(8,128)(2,1)S(1)} %get-tuple-element.7.left_ref, bf16[2,4,2,4,2,64,128]{6,5,4,3,2,1,0:T(8,128)(2,1)S(1)} %get-tuple-element.8.other_ref), custom_call_target="tpu_custom_call" | custom-call | tf_op jit(solution)/shard_map/cross_products/pallas_call | solution.py:293

commit v6 on v3

--- a/solution.py
+++ b/solution.py
@@ -145,8 +145,11 @@
         sorted_ref[step] = sort_part(step)
         swap[step].start()
 
-    for hop in range(hops):
-        for part in range(n_seg):
+    early, late = range(n_seg // 2), range(n_seg // 2, n_seg)
+    visits = [(0, early), (1, early), (0, late), (1, late)]
+    visits += [(hop, parts) for hop in range(2, hops) for parts in (early, late)]
+    for hop, parts in visits:
+        for part in parts:
             if hop == 0 and part > 0:
                 swap[part].wait_recv()
             for way in range(2):
@@ -157,7 +160,7 @@
             if hop > 1:
                 product(hop - 1, part)
                 product(n_chan - hop + 1, part)
-        if hop == 0:
+        if hop == 1 and parts is late:
             make_left()
     for turn in range(turns):
         if hops > 1:
@@ -184,9 +187,8 @@
     for r in range(out_ref.shape[0]):
         away = place + n_chan - ring_place(plan_ref[r, chan], n_chan)
         slot = lax.rem(away, n_chan) - 1
-        for b in range(out_ref.shape[1]):
-            copies.append(pltpu.make_async_copy(product_ref.at[slot, b], out_ref.at[r, b], sem.at[r, b]))
-            copies[-1].start()
+        copies.append(pltpu.make_async_copy(product_ref.at[slot], out_ref.at[r], sem.at[r]))
+        copies[-1].start()
     for copy in copies:
         copy.wait()
 
@@ -233,7 +235,7 @@
         out_shape=jax.ShapeDtypeStruct((rounds, bins, 2, width, width), jnp.float32),
         in_specs=[pl.BlockSpec(memory_space=pltpu.SMEM), pl.BlockSpec(memory_space=pl.ANY)],
         out_specs=pl.BlockSpec(memory_space=pl.ANY),
-        scratch_shapes=[pltpu.SemaphoreType.DMA((rounds, bins))],
+        scratch_shapes=[pltpu.SemaphoreType.DMA((rounds,))],
         compiler_params=pltpu.CompilerParams(vmem_limit_bytes=4 << 20),
         name="choose_products",
     )(plan, products)

time: 49.7 us -> 49.5 us (level)
  no operation moved by 1% of the time
where the time goes in v6:
time: 49.5 us; the launch traced here: 49.4 us
  Pallas kernels  49.3 us (100%)
    pallas_call x1, Pallas kernels, on_device(): pl.pallas_call(functools.partial(cross_ring_kernel, n_chan, n_seg, scale)...  46.7 us
    pallas_call x1, Pallas kernels, on_device(): pl.pallas_call(functools.partial(choose_kernel, n_chan), out_shape=jax.Sh...  2.64 us

profile of v6, /device:TPU:0, one launch (start us, length us, event | category | flops | bytes accessed | tf_op | source)
XLA Modules:
  0.0 49.4 jit_solution(3174243483437253746)
XLA Ops:
  0.0 0.0 copy-start
  0.0 46.7 %cross_ring.1.product_ref = f32[7,8,2,128,128]{4,3,2,1,0:T(8,128)S(1)} custom-call(s32[1,128]{1,0:T(1,128)} %bitcast.3, bf16[32,64,128]{2,1,0:T(8,128)(2,1)} %bitcast.2), custom_call_target="tpu_custom_call" | custom-call | tf_op jit(solution)/shard_map/cross_ring/pallas_call | solution.py:204
  46.7 0.0 copy-done
  46.7 2.6 %choose_products.1 = f32[4,8,2,128,128]{4,3,2,1,0:T(8,128)} custom-call(s32[4,8]{1,0:T(4,128)S(1)} %copy-done, f32[7,8,2,128,128]{4,3,2,1,0:T(8,128)S(1)} %cross_ring.1.product_ref), custom_call_target="tpu_custom_call" | custom-call | tf_op jit(solution)/shard_map/choose_products/pallas_call | solution.py:233
Async XLA Ops:
  0.0 46.7 %copy-start = (s32[4,8]{1,0:T(4,128)S(1)}, s32[4,8]{1,0:T(4,128)}, u32[]{:S(2)}) copy-start(s32[4,8]{1,0:T(4,128)} %plan_ref.1) | copy-start | bytes 388

commit v7 on v6

--- a/solution.py
+++ b/solution.py
@@ -28,9 +28,9 @@
 
 
 def cross_ring_kernel(
-    n_chan, n_seg, scale, slots_ref, x_ref, out_ref,
+    n_chan, n_seg, scale, slots_ref, x_ref, out_ref, left_out_ref, last_ref,
     assign_ref, assign_sem, entry_ref, sorted_ref, block_ref, left_ref, stage_ref,
-    entry_sem, stage_sem, seg_send, seg_recv, ring_send, ring_recv,
+    entry_sem, stage_sem, left_sem, last_sem, seg_send, seg_recv, ring_send, ring_recv,
 ):
     chan, seg = lax.axis_index("chan"), lax.axis_index("seg")
     place = ring_place(chan, n_chan)
@@ -119,6 +119,11 @@
             left_ref[b, :width] = x.T
             left_ref[b, width:] = turned.astype(jnp.bfloat16).T
 
+    left = pltpu.make_async_copy(left_ref, left_out_ref, left_sem)
+    last = [
+        pltpu.make_async_copy(block_ref.at[hops, part], last_ref.at[part], last_sem.at[part])
+        for part in range(n_seg)
+    ]
     leaving = {}
     stages = stage_ref.shape[0]
 
@@ -162,6 +167,7 @@
                 product(n_chan - hop + 1, part)
         if hop == 1 and parts is late:
             make_left()
+            left.start()
     for turn in range(turns):
         if hops > 1:
             product(hops - 1, turn)
@@ -170,25 +176,34 @@
         for way in range(2):
             if (way, hops - 1, part) in ring:
                 ring[way, hops - 1, part].wait_recv()
-    for turn in range(turns):
-        product(hops, turn)
+        last[part].start()
+    left.wait()
     for step in range(1, n_seg):
         swap[step].wait_send()
     for copy in ring.values():
         copy.wait_send()
-    for copy in leaving.values():
+    for copy in list(leaving.values()) + last:
         copy.wait()
 
 
-def choose_kernel(n_chan, plan_ref, product_ref, out_ref, sem):
+def choose_kernel(n_chan, scale, plan_ref, product_ref, left_ref, last_ref, out_ref, made_ref, sem):
     chan = lax.axis_index("chan")
     place = ring_place(chan, n_chan)
-    copies = []
+    parts, bins, rows, width = last_ref.shape
+    hops = n_chan // 2
+    slots, copies, mades = [], [], []
     for r in range(out_ref.shape[0]):
         away = place + n_chan - ring_place(plan_ref[r, chan], n_chan)
-        slot = lax.rem(away, n_chan) - 1
-        copies.append(pltpu.make_async_copy(product_ref.at[slot], out_ref.at[r], sem.at[r]))
-        copies[-1].start()
+        slots.append(lax.rem(away, n_chan))
+        copies.append(pltpu.make_async_copy(product_ref.at[slots[r] - 1], out_ref.at[r], sem.at[r]))
+        mades.append(pltpu.make_async_copy(made_ref, out_ref.at[r], sem.at[r]))
+        pl.when(slots[r] != hops)(copies[r].start)
+    for b in range(bins):
+        y = last_ref[:, b].reshape(parts * rows, width)
+        both = jnp.dot(left_ref[b], y, preferred_element_type=jnp.float32) * scale
+        made_ref[b] = both.reshape(2, width, width)
+    for r in range(out_ref.shape[0]):
+        pl.when(slots[r] == hops)(mades[r].start)
     for copy in copies:
         copy.wait()
 
@@ -201,11 +216,15 @@
     hops = n_chan // 2
     part = (n_seg, bins, rows, width)
     spent = 2 * n_chan * n_seg * bins * rows * width
-    products = pl.pallas_call(
+    products, lefts, last = pl.pallas_call(
         functools.partial(cross_ring_kernel, n_chan, n_seg, scale),
-        out_shape=jax.ShapeDtypeStruct((n_chan - 1, bins, 2, width, width), jnp.float32),
+        out_shape=(
+            jax.ShapeDtypeStruct((n_chan - 1, bins, 2, width, width), jnp.float32),
+            jax.ShapeDtypeStruct((bins, 2 * width, n_seg * rows), jnp.bfloat16),
+            jax.ShapeDtypeStruct(part, jnp.bfloat16),
+        ),
         in_specs=[pl.BlockSpec(memory_space=pltpu.HBM)] * 2,
-        out_specs=pl.BlockSpec(memory_space=pl.ANY),
+        out_specs=[pl.BlockSpec(memory_space=pl.ANY)] * 3,
         scratch_shapes=[
             pltpu.VMEM((1, width), jnp.int32),
             pltpu.SemaphoreType.DMA,
@@ -216,6 +235,8 @@
             pltpu.VMEM((4, bins, 2, width, width), jnp.float32),
             pltpu.SemaphoreType.DMA((n_seg,)),
             pltpu.SemaphoreType.DMA((4, n_seg)),
+            pltpu.SemaphoreType.DMA,
+            pltpu.SemaphoreType.DMA((n_seg,)),
             pltpu.SemaphoreType.DMA((n_seg,)),
             pltpu.SemaphoreType.DMA((n_seg,)),
             pltpu.SemaphoreType.DMA((2, hops, n_seg)),
@@ -231,14 +252,22 @@
     )
 
     return pl.pallas_call(
-        functools.partial(choose_kernel, n_chan),
+        functools.partial(choose_kernel, n_chan, scale),
         out_shape=jax.ShapeDtypeStruct((rounds, bins, 2, width, width), jnp.float32),
-        in_specs=[pl.BlockSpec(memory_space=pltpu.SMEM), pl.BlockSpec(memory_space=pl.ANY)],
+        in_specs=[
+            pl.BlockSpec(memory_space=pltpu.SMEM),
+            pl.BlockSpec(memory_space=pl.ANY),
+            pl.BlockSpec(memory_space=pltpu.VMEM),
+            pl.BlockSpec(memory_space=pltpu.VMEM),
+        ],
         out_specs=pl.BlockSpec(memory_space=pl.ANY),
-        scratch_shapes=[pltpu.SemaphoreType.DMA((rounds,))],
-        compiler_params=pltpu.CompilerParams(vmem_limit_bytes=4 << 20),
+        scratch_shapes=[
+            pltpu.VMEM((bins, 2, width, width), jnp.float32),
+            pltpu.SemaphoreType.DMA((rounds,)),
+        ],
+        compiler_params=pltpu.CompilerParams(vmem_limit_bytes=8 << 20),
         name="choose_products",
-    )(plan, products)
+    )(plan, products, lefts, last)
 
 
 def solution(mesh):

time: 49.5 us -> 50.1 us (1.012)
  local copies, waits for them, and re-layouts: 0.01 us -> 0.68 us
    unnamed x2, local copies, waits for them, and re-layouts: 0.01 us -> 0.68 us
where the time goes in v7:
time: 50.1 us; the launch traced here: 49.9 us
  Pallas kernels  49.2 us (98%)
  local copies, waits for them, and re-layouts  0.68 us (1%)
    pallas_call x1, Pallas kernels, on_device(): pl.pallas_call(functools.partial(cross_ring_kernel, n_chan, n_seg, scale)...  46.3 us
    pallas_call x1, Pallas kernels, on_device(): pl.pallas_call(functools.partial(choose_kernel, n_chan, scale), out_shape...  2.93 us

profile of v7, /device:TPU:0, one launch (start us, length us, event | category | flops | bytes accessed | tf_op | source)
XLA Modules:
  0.0 49.9 jit_solution(4646665928708671535)
XLA Ops:
  0.0 46.3 %cross_ring.1 = (f32[7,8,2,128,128]{4,3,2,1,0:T(8,128)S(1)}, bf16[8,256,256]{2,1,0:T(8,128)(2,1)S(1)}, bf16[4,8,64,128]{3,2,1,0:T(8,128)(2,1)S(1)}) custom-call(s32[1,128]{1,0:T(1,128)} %bitcast.3, bf16[32,64,128]{2,1,0:T(8,128)(2,1)} %bitcast.2), custom_call_target="tpu_custom_call" | custom-call | tf_op jit(solution)/shard_map/cross_ring/pallas_call | solution.py:219
  46.3 0.0 copy-start
  46.3 0.7 %copy-done = s32[4,8]{1,0:T(4,128)S(1)} copy-done((s32[4,8]{1,0:T(4,128)S(1)}, s32[4,8]{1,0:T(4,128)}, u32[]{:S(2)}) %copy-start) | copy-done | bytes 152
  47.0 2.9 %choose_products.1 = f32[4,8,2,128,128]{4,3,2,1,0:T(8,128)} custom-call(s32[4,8]{1,0:T(4,128)S(1)} %copy-done, f32[7,8,2,128,128]{4,3,2,1,0:T(8,128)S(1)} %get-tuple-element.8.product_ref, bf16[8,256,256]{2,1,0:T(8,128)(2,1)S(1)} %get-tuple-element.9.left_ref, bf16[4,8,64,128]{3,2,1,0:T(8,128)(2,1)S(1)} %get-tuple-element.10.last_ref), custom_call_target="tpu_custom_call" | custom-call | tf_op jit(solution)/shard_map/choose_products/pallas_call | solution.py:254
Async XLA Ops:
  46.3 0.7 %copy-start = (s32[4,8]{1,0:T(4,128)S(1)}, s32[4,8]{1,0:T(4,128)}, u32[]{:S(2)}) copy-start(s32[4,8]{1,0:T(4,128)} %plan_ref.1) | copy-start | bytes 388

commit v8 on v6

--- a/solution.py
+++ b/solution.py
@@ -76,9 +76,10 @@
     def ring_copy(way, hop, part):
         held = (n_chan - hop) % n_chan if way else hop
         lands = n_chan - hop - 1 if way else hop + 1
+        some = pl.ds(part, n_seg // 2 if hop else 1)
         return pltpu.make_async_remote_copy(
-            src_ref=block_ref.at[held, part],
-            dst_ref=block_ref.at[lands, part],
+            src_ref=block_ref.at[held, some],
+            dst_ref=block_ref.at[lands, some],
             send_sem=ring_send.at[way, hop, part],
             recv_sem=ring_recv.at[way, hop, part],
             device_id=(sides[way], seg),
@@ -86,6 +87,8 @@
         )
 
     def goes(way, hop, part):
+        if hop and part % (n_seg // 2):
+            return False
         return hop < hops - 1 or (part >= n_seg // 2) == bool(way)
 
     ring = {
@@ -153,7 +156,10 @@
             if hop == 0 and part > 0:
                 swap[part].wait_recv()
             for way in range(2):
-                if hop > 0 and (way, hop - 1, part) in ring:
+                if hop == 1 and part == parts[0]:
+                    for each in parts:
+                        ring[way, 0, each].wait_recv()
+                if hop > 1 and (way, hop - 1, part) in ring:
                     ring[way, hop - 1, part].wait_recv()
                 if (way, hop, part) in ring and (hop, part) != (0, 0):
                     ring[way, hop, part].start()

time: 49.5 us -> 53.8 us (1.087)
  Pallas kernels: 49.3 us -> 53.6 us
    pallas_call x1, Pallas kernels: 46.7 us -> 51 us  [on_device(): pl.pallas_call(functools.partial(cross_ring_kernel, n_chan, n_seg, scale)...]
where the time goes in v8:
time: 53.8 us; the launch traced here: 53.6 us
  Pallas kernels  53.6 us (100%)
    pallas_call x1, Pallas kernels, on_device(): pl.pallas_call(functools.partial(cross_ring_kernel, n_chan, n_seg, scale)...  51 us
    pallas_call x1, Pallas kernels, on_device(): pl.pallas_call(functools.partial(choose_kernel, n_chan), out_shape=jax.Sh...  2.64 us

profile of v8, /device:TPU:0, one launch (start us, length us, event | category | flops | bytes accessed | tf_op | source)
XLA Modules:
  0.0 53.6 jit_solution(14941433759042362778)
XLA Ops:
  0.0 0.0 copy-start
  0.0 51.0 %cross_ring.1.product_ref = f32[7,8,2,128,128]{4,3,2,1,0:T(8,128)S(1)} custom-call(s32[1,128]{1,0:T(1,128)} %bitcast.3, bf16[32,64,128]{2,1,0:T(8,128)(2,1)} %bitcast.2), custom_call_target="tpu_custom_call" | custom-call | tf_op jit(solution)/shard_map/cross_ring/pallas_call | solution.py:210
  51.0 0.0 copy-done
  51.0 2.6 %choose_products.1 = f32[4,8,2,128,128]{4,3,2,1,0:T(8,128)} custom-call(s32[4,8]{1,0:T(4,128)S(1)} %copy-done, f32[7,8,2,128,128]{4,3,2,1,0:T(8,128)S(1)} %cross_ring.1.product_ref), custom_call_target="tpu_custom_call" | custom-call | tf_op jit(solution)/shard_map/choose_products/pallas_call | solution.py:239
Async XLA Ops:
  0.0 51.0 %copy-start = (s32[4,8]{1,0:T(4,128)S(1)}, s32[4,8]{1,0:T(4,128)}, u32[]{:S(2)}) copy-start(s32[4,8]{1,0:T(4,128)} %plan_ref.1) | copy-start | bytes 388
